TPU v7x, 1024 devices: a whole 8x8x8 slice. The times are simulated.
1024 devices in a mesh: dp: 128 (over y, x, core), fsdp: 8 (over z).
Axes of the slice: x: 8, y: 8, z: 8, core: 2. Of those that a mesh axis runs over, the one named last changes fastest.
Arguments:
- tokens: bfloat16 [65536, 8192], P('dp', 'fsdp'), may hold values from -6 to 6
- frozen_value_weight: bfloat16 [8192, 512], P('fsdp'), may hold values from -0.0625 to 0.0625
- down_factor_rows: bfloat16 [512, 8192], P(None, 'fsdp'), may hold values from -6 to 6
- up_factor_rows: bfloat16 [512, 512], P(None, 'fsdp'), may hold values from -6 to 6
- cotangent: bfloat16 [65536, 512], P('dp', 'fsdp'), may hold values from -6 to 6
- row_adapter_index: int32 [65536, 1], P('dp'), may hold values from 0 to 31
- down_master_copy: float32 [512, 8192], P('dp', 'fsdp'), may hold values from -0.4375 to 0.4375
- up_master_copy: float32 [512, 512], P('dp', 'fsdp'), may hold values from -0.4375 to 0.4375
- down_first_moment: float32 [512, 8192], P('dp', 'fsdp'), may hold values from -0.005859375 to 0.005859375
- down_second_moment: float32 [512, 8192], P('dp', 'fsdp'), may hold values from 5.722046e-09 to 5.7220458e-08
- up_first_moment: float32 [512, 512], P('dp', 'fsdp'), may hold values from -0.0234375 to 0.0234375
- up_second_moment: float32 [512, 512], P('dp', 'fsdp'), may hold values from 9.1552735e-08 to 9.155273e-07
Outputs:
- mixed: bfloat16 [65536, 512], P('dp', 'fsdp')
- new_master_a: float32 [512, 8192], P('dp', 'fsdp')
- new_master_b: float32 [512, 512], P('dp', 'fsdp')
- new_first_a: float32 [512, 8192], P('dp', 'fsdp')
- new_second_a: float32 [512, 8192], P('dp', 'fsdp')
- new_first_b: float32 [512, 512], P('dp', 'fsdp')
- new_second_b: float32 [512, 512], P('dp', 'fsdp')
- returned_a: bfloat16 [512, 8192], P(None, 'fsdp')
- returned_b: bfloat16 [512, 512], P(None, 'fsdp')
Inputs may be any that keep to these rules, and one draw needn't show every extreme that they name: `row_adapter_index`: every adapter names some row.
All inputs are finite; a program needn't handle non-finite values.
Results may differ from a plain program's by a relative error of at most 0.0042.
Values may be sent and summed in bfloat16 or wider, within the bound.
A program may use at most 32 MiB of HBM per device.

v0:
```python
import jax
import jax.numpy as jnp
from jax import lax
from jax.sharding import PartitionSpec as P

MODEL_WIDTH = 8192
RANK = 16
LOCAL_ADAPTERS = 32
STEP = 10


BETA_ONE = 0.9
BETA_TWO = 0.999
ADAM_EPS = 1e-08
LEARN_RATE = 0.01


def select_ranks(values, member):
    total = values.shape[0]
    return jnp.sum((values * member).reshape(total, LOCAL_ADAPTERS, RANK), axis=1)


def adam_step(master, moment_one, moment_two, gradient):
    new_one = BETA_ONE * moment_one + (1.0 - BETA_ONE) * gradient
    new_two = BETA_TWO * moment_two + (1.0 - BETA_TWO) * gradient * gradient
    fix_one = 1.0 - BETA_ONE**STEP
    fix_two = 1.0 - BETA_TWO**STEP
    update = new_one / fix_one / (jnp.sqrt(new_two / fix_two) + ADAM_EPS)
    return (master - LEARN_RATE * update, new_one, new_two)


def shards(
    tokens,
    frozen_value_weight,
    down_factor_rows,
    up_factor_rows,
    cotangent,
    row_adapter_index,
    down_master_copy,
    up_master_copy,
    down_first_moment,
    down_second_moment,
    up_first_moment,
    up_second_moment,
):
    input_scale = 1.0 / MODEL_WIDTH**0.5
    adapter_of = row_adapter_index[:, 0]
    onehot = (adapter_of[:, None] == jnp.arange(LOCAL_ADAPTERS, dtype=jnp.int32)[None, :]).astype(
        jnp.float32
    )
    member = jnp.repeat(onehot, RANK, axis=1)
    base_part = jnp.dot(tokens, frozen_value_weight, preferred_element_type=jnp.float32)
    projected_rows = (
        lax.dot_general(
            tokens, down_factor_rows, (((1,), (1,)), ((), ())), preferred_element_type=jnp.float32
        )
        * input_scale
    )
    rank_part = select_ranks(projected_rows, member)
    backward_pass = lax.dot_general(
        cotangent, up_factor_rows, (((1,), (1,)), ((), ())), preferred_element_type=jnp.float32
    )
    grad_part = 0.25 * select_ranks(backward_pass, member)
    own_width = cotangent.shape[1]
    base_total, rank_total, grad_total = lax.psum((base_part, rank_part, grad_part), "fsdp")
    offset = lax.axis_index("fsdp") * own_width
    base_local_output = lax.dynamic_slice_in_dim(base_total, offset, own_width, 1)
    ranks = rank_total.astype(jnp.bfloat16)
    spread_rows = (jnp.tile(ranks.astype(jnp.float32), (1, LOCAL_ADAPTERS)) * member).astype(
        jnp.bfloat16
    )
    mixed = (
        base_local_output
        + 0.25 * jnp.dot(spread_rows, up_factor_rows, preferred_element_type=jnp.float32)
    ).astype(jnp.bfloat16)
    rank_grads = grad_total.astype(jnp.bfloat16)
    grad_spread = (jnp.tile(rank_grads.astype(jnp.float32), (1, LOCAL_ADAPTERS)) * member).astype(
        jnp.bfloat16
    )
    grad_a_part = (
        lax.dot_general(
            grad_spread, tokens, (((0,), (0,)), ((), ())), preferred_element_type=jnp.float32
        )
        * input_scale
    )
    grad_b_part = 0.25 * lax.dot_general(
        spread_rows, cotangent, (((0,), (0,)), ((), ())), preferred_element_type=jnp.float32
    )
    count_part = jnp.sum(member, axis=0)
    grad_a_sum, grad_b_sum, counts = (
        lax.psum_scatter(grad_a_part, "dp", scatter_dimension=0, tiled=True),
        lax.psum_scatter(grad_b_part, "dp", scatter_dimension=0, tiled=True),
        lax.psum_scatter(count_part, "dp", scatter_dimension=0, tiled=True),
    )
    grad_a = grad_a_sum / counts[:, None]
    grad_b = grad_b_sum / counts[:, None]
    new_master_a, new_first_a, new_second_a = adam_step(
        down_master_copy, down_first_moment, down_second_moment, grad_a
    )
    new_master_b, new_first_b, new_second_b = adam_step(
        up_master_copy, up_first_moment, up_second_moment, grad_b
    )
    returned_a, returned_b = (
        lax.all_gather(new_master_a.astype(jnp.bfloat16), "dp", axis=0, tiled=True),
        lax.all_gather(new_master_b.astype(jnp.bfloat16), "dp", axis=0, tiled=True),
    )
    return (
        mixed,
        new_master_a,
        new_master_b,
        new_first_a,
        new_second_a,
        new_first_b,
        new_second_b,
        returned_a,
        returned_b,
    )


def solution(mesh):
    return jax.shard_map(
        shards,
        mesh=mesh,
        in_specs=(
            P("dp", "fsdp"),
            P("fsdp", None),
            P(None, "fsdp"),
            P(None, "fsdp"),
            P("dp", "fsdp"),
            P("dp", None),
            P("dp", "fsdp"),
            P("dp", "fsdp"),
            P("dp", "fsdp"),
            P("dp", "fsdp"),
            P("dp", "fsdp"),
            P("dp", "fsdp"),
        ),
        out_specs=(
            P("dp", "fsdp"),
            P("dp", "fsdp"),
            P("dp", "fsdp"),
            P("dp", "fsdp"),
            P("dp", "fsdp"),
            P("dp", "fsdp"),
            P("dp", "fsdp"),
            P(None, "fsdp"),
            P(None, "fsdp"),
        ),
        check_vma=False,
    )
```

profile of v0, /device:TPU:1, one launch (start us, length us, event | category | flops | bytes accessed | tf_op | source)
XLA Modules:
  0.0 453.1 jit_solution(12066835567414295799)
XLA Ops:
  7.2 0.0 copy-start
  7.2 0.0 copy-start.1
  7.2 0.0 all-reduce.10.cloned.1.call-start
  7.2 0.8 fusion.4
  8.1 1.2 bitcast_multiply_fusion.1
  9.3 0.1 reduce_sum.32
  9.4 0.0 copy-done
  9.4 0.0 copy-done.1
  9.4 0.0 copy-start.2
  9.4 0.7 bitcast_multiply_fusion.3
  10.2 0.1 reduce_sum.31
  10.2 36.6 %all-reduce.4 = (bf16[512,16]{0,1:T(8,128)(2,1)S(1)}, bf16[512,16]{0,1:T(8,128)(2,1)S(1)}) all-reduce(f32[512,16]{0,1:T(8,128)S(1)} %reduce_sum.31, f32[512,16]{0,1:T(8,128)S(1)} %broadcast_multiply_fusion), channel_id=1, replica_groups=mesh['dp'=128,'fsdp'=8] {'fsdp'}, use_global_device_ids=true, to_apply=%region_2.0 | all-reduce | flops 16384 | bytes 98304 | tf_op jit(solution)/shard_map/psum | solution.py:65
  46.9 0.2 fusion.3
  47.1 0.0 copy-done.2
  47.1 1.0 convolution_multiply_fusion.3
  48.0 0.0 copy-start.11
  48.0 2.0 convolution_multiply_fusion
  50.1 0.0 all-reduce.10.cloned.1.call-update
  50.1 0.0 copy-start.7
  50.1 0.0 copy-start.4
  50.1 0.0 copy-start.5
  50.1 0.0 copy-start.6
  50.1 0.0 copy-start.3
  50.2 0.0 copy-start.8
  50.2 0.0 copy-start.9
  50.2 0.0 copy-start.10
  50.2 0.0 all-reduce.8.cloned.1.call-start
  50.2 0.0 copy-done.11
  50.3 1.7 fusion.10
  52.0 0.0 all-reduce.8.cloned.1.call-update
  52.0 0.0 all-gather.4.cloned.1.call-start
  52.1 0.0 copy-done.7
  52.1 0.1 fusion.5
  52.2 0.1 reduce_sum.34
  52.3 0.1 reduce_sum.35
  52.3 1.3 dynamic-slice
  54.3 255.9 %all-reduce.1 = f32[512]{0:T(512)S(1)} all-reduce(f32[512]{0:T(512)S(1)} %reduce_sum.35), channel_id=3, replica_groups=mesh['dp'=128,'fsdp'=8] {'dp'}, use_global_device_ids=true, to_apply=%region_7.0.clone | all-reduce | flops 512 | bytes 4096
  310.2 0.1 dynamic-slice.3
  310.2 0.0 all-reduce.10.cloned.1.call-done
  310.2 0.0 copy-done.4
  310.2 0.0 copy-done.5
  310.2 0.0 copy-done.6
  310.3 1.5 convert_bitcast_fusion
  311.7 0.0 all-gather.4.cloned.1.call-update
  311.8 41.3 %all-reduce.8.cloned.1.call-done = f32[512,512]{0,1:T(8,128)} async-done(((f32[512,512]{0,1:T(8,128)}), f32[512,512]{0,1:T(8,128)}) %all-reduce.8.cloned.1.call-update) | async-done | bytes 1048592 | tf_op jit(solution)/shard_map/psum | solution.py:65
  353.0 0.0 copy-done.3
  353.0 1.7 fusion.1
  354.8 0.8 constant_dynamic-slice_fusion
  355.6 0.1 copy.53
  355.7 0.0 copy-done.8
  355.7 0.0 copy-done.9
  355.7 0.0 copy-done.10
  355.7 0.7 convert_bitcast_fusion.1
  356.4 55.0 %all-gather.1 = bf16[128,4,64]{2,1,0:T(4,128)(2,1)S(1)} all-gather(bf16[1,4,64]{2,1,0:T(4,128)(2,1)S(1)} %get-tuple-element.49), channel_id=1, replica_groups=mesh['dp'=128,'fsdp'=8] {'dp'}, dimensions={0}, use_global_device_ids=true | all-gather | bytes 66048 | tf_op jit(solution)/shard_map/all_gather | solution.py:105
  411.4 0.7 copy.54
  412.1 32.3 %all-gather.4.cloned.1.call-done = bf16[128,4,1024]{2,1,0:T(4,128)(2,1)} async-done(((bf16[1,4,1024]{2,1,0:T(4,128)(2,1)}), bf16[128,4,1024]{2,1,0:T(4,128)(2,1)}) %all-gather.4.cloned.1.call-update) | async-done | bytes 1048592 | tf_op jit(solution)/shard_map/all_gather | solution.py:104
  444.4 2.1 reshape.41
  (3 shorter events, 0.0 us)
Async XLA Ops:
  7.2 2.2 copy-start
  7.2 2.2 copy-start.1
  7.2 303.0 %all-reduce.10.cloned.1.call-start = ((), (), s32[]{:S(2)}) async-start(), calls=%async_computation.2 | async-start | bytes 4456448
  9.4 37.7 %copy-start.2 = (bf16[512,64]{0,1:T(8,128)(2,1)S(1)}, bf16[512,64]{0,1:T(8,128)(2,1)}, u32[]{:S(2)}) copy-start(bf16[512,64]{0,1:T(8,128)(2,1)} %param.16) | copy-start | bytes 196612
  48.0 2.2 copy-start.11
  50.1 2.0 copy-start.7
  50.1 260.1 %copy-start.4 = (f32[4,1024]{1,0:T(4,128)S(1)}, f32[4,1024]{1,0:T(4,128)}, u32[]{:S(2)}) copy-start(f32[4,1024]{1,0:T(4,128)} %param.18) | copy-start | bytes 49156
  50.1 260.1 %copy-start.5 = (f32[4,1024]{1,0:T(4,128)S(1)}, f32[4,1024]{1,0:T(4,128)}, u32[]{:S(2)}) copy-start(f32[4,1024]{1,0:T(4,128)} %param.20) | copy-start | bytes 49156
  50.1 260.1 %copy-start.6 = (f32[4,1024]{1,0:T(4,128)S(1)}, f32[4,1024]{1,0:T(4,128)}, u32[]{:S(2)}) copy-start(f32[4,1024]{1,0:T(4,128)} %param.21) | copy-start | bytes 49156
  50.1 302.9 %copy-start.3 = (bf16[512,64]{0,1:T(8,128)(2,1)S(1)}, bf16[512,64]{0,1:T(8,128)(2,1)}, u32[]{:S(2)}) copy-start(bf16[512,64]{0,1:T(8,128)(2,1)} %param.15) | copy-start | bytes 196612
  50.2 305.5 %copy-start.8 = (f32[4,64]{1,0:T(4,128)S(1)}, f32[4,64]{1,0:T(4,128)}, u32[]{:S(2)}) copy-start(f32[4,64]{1,0:T(4,128)} %param.19) | copy-start | bytes 3076
  50.2 305.5 %copy-start.9 = (f32[4,64]{1,0:T(4,128)S(1)}, f32[4,64]{1,0:T(4,128)}, u32[]{:S(2)}) copy-start(f32[4,64]{1,0:T(4,128)} %param.22) | copy-start | bytes 3076
  50.2 305.5 %copy-start.10 = (f32[4,64]{1,0:T(4,128)S(1)}, f32[4,64]{1,0:T(4,128)}, u32[]{:S(2)}) copy-start(f32[4,64]{1,0:T(4,128)} %param.23) | copy-start | bytes 3076
  50.2 302.8 %all-reduce.8.cloned.1.call-start = ((), (), s32[]{:S(2)}) async-start(), calls=%async_computation | async-start | bytes 2097152 | tf_op jit(solution)/shard_map/psum | solution.py:65
  52.0 392.4 %all-gather.4.cloned.1.call-start = ((), (), s32[]{:S(2)}) async-start(), calls=%async_computation.1 | async-start | bytes 1056768 | tf_op jit(solution)/shard_map/all_gather | solution.py:104
Sparse Core Ops, SparseCore 0:
  50.2 215.5 all-reduce.9
  268.8 84.1 all-reduce.7
  358.0 86.4 all-gather.3
where the time goes:
time: 454 us; the launch traced here: 453 us
  blocking collectives  348 us (77%)
  waiting for transfers between devices  73.6 us (16%)
  between operations  14.6 us (3%)
  matrix products  8.41 us (2%)
  local copies, waits for them, and re-layouts  5.35 us (1%)
    unnamed x1, blocking collectives  256 us
    all_gather x1, blocking collectives, shards(): lax.all_gather(new_master_b.astype(jnp.bfloat16), 'dp', axis=0, tiled=True)  55 us
    psum x1, waiting for transfers between devices, shards(): lax.psum((base_part, rank_part, grad_part), 'fsdp')  41.3 us
    psum x1, blocking collectives, shards(): lax.psum((base_part, rank_part, grad_part), 'fsdp')  36.6 us
    all_gather x1, waiting for transfers between devices, shards(): lax.all_gather(new_master_a.astype(jnp.bfloat16), 'dp', axis=0, tiled=True)  32.3 us
  transfers between devices with their start and end apart: 3, of which 2 were waited for; matrix products, arithmetic and copies ran while one was open for 2% of the time, Pallas kernels for 0%

commit v1 on v0

v1 whole, which is shorter than its diff:
```python
import functools

import jax
import jax.numpy as jnp
from jax import lax
from jax.experimental import pallas as pl
from jax.experimental.pallas import tpu as pltpu
from jax.sharding import PartitionSpec as P

YS, XS, ZS = 8, 8, 8
MODEL_WIDTH = 8192
RANK = 16
STEP = 10
BETA_ONE = 0.9
BETA_TWO = 0.999
ADAM_EPS = 1e-08
LEARN_RATE = 0.01
SCALE = 1.0 / MODEL_WIDTH**0.5

MESH = pl.DeviceIdType.MESH
F32 = jnp.float32
BF16 = jnp.bfloat16
T = 512
D = 1024
Q = 64
LANES = 128


def adam_step(master, moment_one, moment_two, gradient):
    new_one = BETA_ONE * moment_one + (1.0 - BETA_ONE) * gradient
    new_two = BETA_TWO * moment_two + (1.0 - BETA_TWO) * gradient * gradient
    fix_one = 1.0 - BETA_ONE**STEP
    fix_two = 1.0 - BETA_TWO**STEP
    update = new_one / fix_one / (jnp.sqrt(new_two / fix_two) + ADAM_EPS)
    return (master - LEARN_RATE * update, new_one, new_two)


def far_first(n):
    return sorted(range(1, n), key=lambda k: -min(k, n - k))


def scratch(ys, xs, zs):
    ms = xs // 2
    nb = ms // 2
    c = ys * ms * RANK
    bz = 8 // zs
    v = pltpu.VMEM
    dma = pltpu.SemaphoreType.DMA
    bufs = dict(
        tok=v((T, D), BF16),
        down=v((c, D), BF16),
        w=v((D, zs * Q), BF16),
        proj=v((c, T), F32),
        spread_r=v((c, T), BF16),
        spread_g=v((c, T), BF16),
        gx=v((zs, bz * 8, LANES), F32),
        gr=v((zs, bz * 8, LANES), F32),
        gg=v((zs, bz * 8, LANES), F32),
        rx=v((zs, bz * 8, LANES), F32),
        rr=v((zs, bz * 8, LANES), F32),
        rg=v((zs, bz * 8, LANES), F32),
        bx=v((zs, T // 2, LANES), BF16),
        br=v((zs, T // 2, LANES), BF16),
        c0=v((8, LANES), F32),
        c0r=v((8, LANES), F32),
        c1=v((8, LANES), F32),
        c1r=v((xs, 8, LANES), F32),
        c2=v((8, LANES), F32),
        c2r=v((ys, 8, LANES), F32),
        pfx=v((4, 3, 4, 256), F32),
        pfr=v((4, 3, 4, 256), F32),
        sx=v((2, c, 256), F32),
        sr=v((2, c, 256), F32),
        own=v((2, c, 256), F32),
        sbx=v((ys, nb, RANK, LANES), F32),
        sbr=v((ys, nb, RANK, LANES), F32),
        a1x=v((xs, ys, RANK, LANES), BF16),
        a1r=v((xs, ys, RANK, LANES), BF16),
        a2x=v((ys, RANK, LANES), F32),
        a2r=v((ys, RANK, LANES), F32),
        b1x=v((ys, xs + nb, RANK, LANES), BF16),
        b1r=v((ys, xs + nb, RANK, LANES), BF16),
        b2x=v((xs, 2, RANK, LANES), F32),
        b2r=v((xs, 2, RANK, LANES), F32),
        g4=v((4, 4, 256), F32),
        g4r=v((4, 4, 256), F32),
        bq=v((4, 4, Q), F32),
        tile_b=v((RANK, LANES), BF16),
        rows=v((ys, ms, RANK, D), BF16),
        bg=v((xs, RANK, LANES), BF16),
        bt=v((ys, nb, RANK, LANES), BF16),
        bs=v((ys, nb, RANK, LANES), BF16),
        ball=v((c, LANES), F32),
    )
    sems = dict(
        load=3, gz1=zs, gz2=zs, rz1=zs, rz2=zs, bz=zs, cc=1, cx=xs, cy=ys, pf=4, sib=3,
        a1=xs, b1=ys, a2=ys, b2=xs, ret=4, ay=ys, ax=xs, bx_=xs, by=ys, bbx=xs, bby=ys, bbs=1,
        fa=xs, fb=ys, out=1,
    )
    local = ("load", "out")
    order = list(bufs)
    shapes = list(bufs.values())
    for name, n in sems.items():
        order.append(name + "_s")
        shapes.append(dma((n,)))
        if name not in local:
            order.append(name + "_r")
            shapes.append(dma((n,)))
    return order, shapes


INPUTS = ("tok_h", "w_h", "down_h", "up", "cot", "idx", "ma", "mb", "fa_", "sa", "fb_", "sb")
OUTPUTS = ("mixed", "nma", "nmb", "nfa", "nsa", "nfb", "nsb", "reta", "retb")


class Refs:
    def __init__(self, names, refs):
        self.__dict__.update(zip(names, refs))


def kernel(ys, xs, zs, order, *refs):
    r = Refs(INPUTS + OUTPUTS + tuple(order), refs)
    ms = xs // 2
    nb = ms // 2
    na = ys * ms
    c_rows = na * RANK
    bz = 8 // zs
    dp, z = lax.axis_index("dp"), lax.axis_index("fsdp")
    core = dp % 2
    x = (dp // 2) % xs
    y = dp // (2 * xs)
    h, m = x % 2, x // 2
    q = 2 * h + core
    half = core * (D // 2)
    other_half = (1 - core) * (D // 2)

    def at(yy=None, xx=None, cc=None, zz=None):
        yy = y if yy is None else yy
        xx = x if xx is None else xx
        cc = core if cc is None else cc
        return ((yy * xs + xx) * 2 + cc, z if zz is None else zz)

    started = []

    def send(src, dst, name, slot, device):
        copy = pltpu.make_async_remote_copy(
            src_ref=src,
            dst_ref=dst,
            send_sem=getattr(r, name + "_s").at[slot],
            recv_sem=getattr(r, name + "_r").at[slot],
            device_id=device,
            device_id_type=MESH,
        )
        copy.start()
        started.append(copy)
        return copy

    def xp(k):
        return lax.rem(x + k, xs)

    def yp(k):
        return lax.rem(y + k, ys)

    def zp(k):
        return lax.rem(z + k, zs)

    def from_x(k):
        return lax.rem(x + xs - k, xs)

    def from_y(k):
        return lax.rem(y + ys - k, ys)

    sibling = at(cc=1 - core)
    kx, ky, kz = far_first(xs), far_first(ys), far_first(zs)

    load_tok = pltpu.make_async_copy(r.tok_h, r.tok, r.load_s.at[0])
    load_down = pltpu.make_async_copy(r.down_h, r.down, r.load_s.at[1])
    load_w = pltpu.make_async_copy(r.w_h, r.w, r.load_s.at[2])
    load_down.start()
    load_tok.start()
    load_w.start()

    barrier = pltpu.get_barrier_semaphore()
    partners = [at(zz=zp(k)) for k in kz] + [at(xx=xp(k)) for k in kx] + [at(yy=yp(k)) for k in ky]
    x_pair = x + 1 - 2 * h
    partners += [sibling, at(xx=x_pair, cc=1 - core)]
    for device in partners:
        pl.semaphore_signal(barrier, inc=1, device_id=device, device_id_type=MESH)

    idx = r.idx[...]
    idx16 = jnp.broadcast_to(idx, (RANK, T))

    def chosen(values):
        total = jnp.zeros((RANK, T), F32)
        for a in range(na):
            total = jnp.where(idx16 == a, values[a * RANK : (a + 1) * RANK, :], total)
        return total

    def to_blocks(values, ref):
        for b in range(8):
            kh, tb = b // 4, b % 4
            ref[b // bz, (b % bz) * 8 : (b % bz) * 8 + 8, :] = values[
                kh * 8 : kh * 8 + 8, tb * LANES : (tb + 1) * LANES
            ]

    def from_blocks(ref):
        halves = []
        for kh in range(2):
            parts = []
            for tb in range(4):
                b = kh * 4 + tb
                parts.append(ref[b // bz, (b % bz) * 8 : (b % bz) * 8 + 8, :])
            halves.append(jnp.concatenate(parts, axis=1))
        return jnp.concatenate(halves, axis=0)

    def spread_into(values, ref):
        for a in range(na):
            ref[a * RANK : (a + 1) * RANK, :] = jnp.where(idx16 == a, values, 0.0).astype(BF16)

    r.proj[...] = lax.dot_general(
        r.up[...], r.cot[...], (((0,), (0,)), ((), ())), preferred_element_type=F32
    )
    to_blocks(chosen(r.proj), r.gx)
    ids = lax.broadcasted_iota(jnp.int32, (LANES, T), 0)
    onehot = jnp.where(ids == jnp.broadcast_to(idx, (LANES, T)), 1.0, 0.0).astype(BF16)
    counts = lax.dot_general(
        jnp.ones((8, T), BF16), onehot, (((1,), (1,)), ((), ())), preferred_element_type=F32
    )
    r.c0[...] = counts
    for j in range(4):
        hj, cj = j // 2, j % 2
        for i, ref in enumerate((r.ma, r.fa_, r.sa)):
            col = cj * (D // 2) + hj * LANES
            r.pfx[j, i, :, 0:LANES] = ref[:, col : col + LANES]
            r.pfx[j, i, :, LANES : 2 * LANES] = ref[:, col + 256 : col + 256 + LANES]

    pl.semaphore_wait(barrier, len(partners))

    gz1 = [(k, send(r.gx.at[zp(k)], r.gr.at[k], "gz1", k, at(zz=zp(k)))) for k in kz]
    cc = send(r.c0, r.c0r, "cc", 0, sibling)
    pf = []
    for k in range(1, 4):
        hk, ck = k // 2, k % 2
        h2 = h + hk - 2 * h * hk
        c2 = core + ck - 2 * core * ck
        pf.append(
            send(
                r.pfx.at[2 * h2 + c2], r.pfr.at[q], "pf", k, at(xx=2 * m + h2, cc=c2)
            )
        )

    load_down.wait()
    load_tok.wait()
    r.proj[...] = lax.dot_general(
        r.down[...], r.tok[...], (((1,), (1,)), ((), ())), preferred_element_type=F32
    )
    to_blocks(chosen(r.proj), r.rx)
    rz1 = [(k, send(r.rx.at[zp(k)], r.rr.at[k], "rz1", k, at(zz=zp(k)))) for k in kz]

    total = r.gx[z]
    for k, copy in gz1:
        copy.wait_recv()
        total = total + r.gr[k]
    r.gg[z] = (0.25 * total).astype(BF16).astype(F32)
    gz2 = [(k, send(r.gg.at[z], r.gg.at[z], "gz2", k, at(zz=zp(k)))) for k in kz]

    load_w.wait()
    lane = lax.broadcasted_iota(jnp.int32, (T // 2, LANES), 1)
    for i in range(zs // 2):
        part = jnp.dot(
            r.tok[...], r.w[:, i * LANES : (i + 1) * LANES], preferred_element_type=F32
        )
        top, bottom = part[: T // 2], part[T // 2 :]
        r.bx[2 * i] = jnp.where(lane < Q, top, pltpu.roll(bottom, Q, 1)).astype(BF16)
        r.bx[2 * i + 1] = jnp.where(lane < Q, pltpu.roll(top, Q, 1), bottom).astype(BF16)

    total = r.rx[z]
    for k, copy in rz1:
        copy.wait_recv()
        total = total + r.rr[k]
    r.rg[z] = (SCALE * total).astype(BF16).astype(F32)
    rz2 = [(k, send(r.rg.at[z], r.rg.at[z], "rz2", k, at(zz=zp(k)))) for k in kz]

    for _, copy in gz2:
        copy.wait_recv()
    spread_into(from_blocks(r.gg), r.spread_g)
    sib = []
    for part in range(2):
        columns = pl.ds(pl.multiple_of(other_half + part * 256, 256), 256)
        r.sx[part] = jnp.dot(r.spread_g[...], r.tok[:, columns], preferred_element_type=F32)
        sib.append(send(r.sx.at[part], r.sr.at[part], "sib", part, sibling))
    for part in range(2):
        columns = pl.ds(pl.multiple_of(half + part * 256, 256), 256)
        r.own[part] = jnp.dot(r.spread_g[...], r.tok[:, columns], preferred_element_type=F32)

    def chip_sum(part, a, hh):
        rows = slice(a * RANK, (a + 1) * RANK)
        cols = slice(hh * LANES, (hh + 1) * LANES)
        return (r.own[part, rows, cols] + r.sr[part, rows, cols]).astype(BF16)

    sib[0].wait_recv()
    for xx in range(xs):
        for yy in range(ys):
            r.a1x[xx, yy] = chip_sum(0, yy * ms + xx // 2, xx % 2)
    a1 = [(k, send(r.a1x.at[xp(k)], r.a1r.at[k], "a1", k, at(xx=xp(k)))) for k in kx]

    for _, copy in rz2:
        copy.wait_recv()
    spread_into(from_blocks(r.rg), r.spread_r)
    cot2 = jnp.concatenate([r.cot[...], r.cot[...]], axis=0)
    grad_b = lax.dot_general(
        r.spread_r[...], cot2, (((1,), (1,)), ((), ())), preferred_element_type=F32
    )
    lane16 = lax.broadcasted_iota(jnp.int32, (RANK, LANES), 1)
    for yy in range(ys):
        for s in range(nb):
            row = (yy * ms + 2 * s) * RANK
            r.sbx[yy, s] = jnp.where(
                lane16 < Q, grad_b[row : row + RANK], grad_b[row + RANK : row + 2 * RANK]
            )
    sib.append(send(r.sbx, r.sbr, "sib", 2, sibling))

    sib[1].wait_recv()
    for yy in range(ys):
        for xx in range(xs):
            r.b1x[yy, xx] = chip_sum(1, yy * ms + xx // 2, xx % 2)
    sib[2].wait_recv()
    for yy in range(ys):
        for s in range(nb):
            r.b1x[yy, xs + s] = (r.sbx[yy, s] + r.sbr[yy, s]).astype(BF16)
    b1 = [(k, send(r.b1x.at[yp(k)], r.b1r.at[k], "b1", k, at(yy=yp(k)))) for k in ky]

    base = [(k, send(r.bx.at[zp(k)], r.br.at[k], "bz", k, at(zz=zp(k)))) for k in kz]

    cc.wait_recv()
    r.c1[...] = r.c0[...] + r.c0r[...]
    cx = [(k, send(r.c1, r.c1r.at[k], "cx", k, at(xx=xp(k)))) for k in kx]
    total = r.c1[...]
    for k, copy in cx:
        copy.wait_recv()
        total = total + r.c1r[k]
    r.c2[...] = total
    cy = [(k, send(r.c2, r.c2r.at[k], "cy", k, at(yy=yp(k)))) for k in ky]

    for _, copy in a1:
        copy.wait_recv()
    for yy in range(ys):
        total = r.a1x[x, yy].astype(F32)
        for k in kx:
            total = total + r.a1r[k, yy].astype(F32)
        r.a2x[yy] = total
    a2 = [(k, send(r.a2x.at[yp(k)], r.a2r.at[k], "a2", k, at(yy=yp(k)))) for k in ky]
    for _, copy in b1:
        copy.wait_recv()
    sums = []
    for s in range(xs + nb):
        total = r.b1x[y, s].astype(F32)
        for k in ky:
            total = total + r.b1r[k, s].astype(F32)
        sums.append(total)
    for xx in range(xs):
        r.b2x[xx, 0] = sums[xx]
        r.b2x[xx, 1] = sums[xs + xx // 4]
    b2 = [(k, send(r.b2x.at[xp(k)], r.b2r.at[k], "b2", k, at(xx=xp(k)))) for k in kx]

    total = r.c2[...]
    for k, copy in cy:
        copy.wait_recv()
        total = total + r.c2r[k]
    lane8 = lax.broadcasted_iota(jnp.int32, (8, LANES), 1)
    count = jnp.sum(jnp.where(lane8 == y * ms + m, total, 0.0), axis=1, keepdims=True)
    count16 = jnp.concatenate([jnp.broadcast_to(count, (8, LANES))] * 2, axis=0)
    r.pfr[q] = r.pfx[q]
    for copy in pf:
        copy.wait_recv()

    def unit(i, part):
        cols = slice(part * LANES, (part + 1) * LANES)
        return jnp.concatenate([r.pfr[j, i, :, cols] for j in range(4)], axis=0)

    def update_unit(part, total):
        gradient = total * SCALE / count16
        for j in range(4):
            r.g4[j, :, part * LANES : (part + 1) * LANES] = gradient[4 * j : 4 * j + 4]
        new_master, _, _ = adam_step(unit(0, part), unit(1, part), unit(2, part), gradient)
        columns = pl.ds(pl.multiple_of(half + part * 256 + h * LANES, LANES), LANES)
        r.rows[y, m, :, columns] = new_master.astype(BF16)

    cols_a = pl.ds(pl.multiple_of(half + h * LANES, LANES), LANES)
    cols_b = pl.ds(pl.multiple_of(half + 256 + h * LANES, LANES), LANES)
    wide_b = pl.ds(pl.multiple_of(half + 256, 256), 256)

    total = r.a2x[y]
    for k, copy in a2:
        copy.wait_recv()
        total = total + r.a2r[k]
    update_unit(0, total)
    tile = r.rows.at[y, m, :, cols_a]
    ay = [(k, send(tile, tile, "ay", k, at(yy=yp(k)))) for k in ky]

    total = r.b2x[x, 0]
    total_b = r.b2x[x, 1]
    for k, copy in b2:
        copy.wait_recv()
        total = total + r.b2r[k, 0]
        total_b = total_b + r.b2r[k, 1]
    update_unit(1, total)
    tile = r.rows.at[y, m, :, cols_b]
    bx_ = [(k, send(tile, tile, "bx_", k, at(xx=xp(k)))) for k in kx]

    odd = m % 2
    for j in range(4):
        r.bq[j] = jnp.where(
            odd == 1, total_b[4 * j : 4 * j + 4, Q:], total_b[4 * j : 4 * j + 4, :Q]
        )
    gradient = 0.25 * r.bq[q] / count16[:4, :Q]
    new_master, new_first, new_second = adam_step(r.mb[...], r.fb_[...], r.sb[...], gradient)
    r.nmb[...] = new_master
    r.nfb[...] = new_first
    r.nsb[...] = new_second
    wide = jnp.concatenate([new_master, new_master], axis=1)
    lane4 = lax.broadcasted_iota(jnp.int32, (4, LANES), 1)
    wide = jnp.where((lane4 // Q) == odd, wide, 0.0)
    r.bg[x] = jnp.concatenate([jnp.where(q == j, wide, 0.0) for j in range(4)], axis=0).astype(BF16)
    bbx = [(k, send(r.bg.at[x], r.bg.at[x], "bbx", k, at(xx=xp(k)))) for k in kx]

    ret = []
    for k in range(1, 4):
        hk, ck = k // 2, k % 2
        h2 = h + hk - 2 * h * hk
        c2 = core + ck - 2 * core * ck
        ret.append(
            send(r.g4.at[2 * h2 + c2], r.g4r.at[q], "ret", k, at(xx=2 * m + h2, cc=c2))
        )

    for _, copy in ay:
        copy.wait_recv()
    column_a = r.rows.at[:, m, :, cols_a]
    ax = [(k, send(column_a, column_a, "ax", k, at(xx=xp(k)))) for k in kx]
    fa = [send(column_a, column_a, "fa", 0, sibling)]
    for _, copy in bx_:
        copy.wait_recv()
    row_b = r.rows.at[y, :, :, wide_b]
    by = [(k, send(row_b, row_b, "by", k, at(yy=yp(k)))) for k in ky]
    fb = [send(row_b, row_b, "fb", 0, sibling)]
    for _, copy in bbx:
        copy.wait_recv()
    for s in range(nb):
        total = r.bg[4 * s].astype(F32)
        for i in range(1, 4):
            total = total + r.bg[4 * s + i].astype(F32)
        r.bt[y, s] = total.astype(BF16)
    bby = [(k, send(r.bt.at[y], r.bt.at[y], "bby", k, at(yy=yp(k)))) for k in ky]

    r.g4r[q] = r.g4[q]
    for copy in ret:
        copy.wait_recv()
    for j in range(4):
        hj, cj = j // 2, j % 2
        for part in range(2):
            col = cj * (D // 2) + part * 256 + hj * LANES
            cols = slice(col, col + LANES)
            new_master, new_first, new_second = adam_step(
                r.ma[:, cols],
                r.fa_[:, cols],
                r.sa[:, cols],
                r.g4r[j, :, part * LANES : (part + 1) * LANES],
            )
            r.nma[:, cols] = new_master
            r.nfa[:, cols] = new_first
            r.nsa[:, cols] = new_second

    term = jnp.dot(r.up[...], r.spread_r[...], preferred_element_type=F32)
    total = r.bx[z].astype(F32)
    for k, copy in base:
        copy.wait_recv()
        total = total + r.br[k].astype(F32)
    turned = jnp.transpose(total)
    r.mixed[:, : T // 2] = (turned[:Q] + 0.25 * term[:, : T // 2]).astype(BF16)
    r.mixed[:, T // 2 :] = (turned[Q:] + 0.25 * term[:, T // 2 :]).astype(BF16)

    for k, copy in ax:
        copy.wait_recv()
        source = from_x(k)
        region = r.rows.at[
            :,
            source // 2,
            :,
            pl.ds(pl.multiple_of(half + (source % 2) * LANES, LANES), LANES),
        ]
        fa.append(send(region, region, "fa", k, sibling))
    for k, copy in by:
        copy.wait_recv()
        region = r.rows.at[from_y(k), :, :, wide_b]
        fb.append(send(region, region, "fb", k, sibling))
    for _, copy in bby:
        copy.wait_recv()
    bbs = send(r.bt, r.bs, "bbs", 0, sibling)
    for copy in fa + fb:
        copy.wait_recv()
    out = pltpu.make_async_copy(r.rows, r.reta, r.out_s.at[0])
    out.start()
    bbs.wait_recv()
    for yy in range(ys):
        for s in range(nb):
            both = r.bt[yy, s].astype(F32) + r.bs[yy, s].astype(F32)
            row = (yy * ms + 2 * s) * RANK
            r.ball[row : row + RANK, :] = both
            r.ball[row + RANK : row + 2 * RANK, :] = pltpu.roll(both, Q, 1)
    r.retb[...] = jnp.transpose(r.ball[...])[:Q].astype(BF16)
    out.wait()
    for copy in started:
        copy.wait_send()


def shards(ys, xs, zs, tok, w, down, up, cot, idx, ma, mb, fa, sa, fb, sb):
    ms = xs // 2
    c_rows = ys * ms * RANK
    order, shapes = scratch(ys, xs, zs)
    vmem = pl.BlockSpec(memory_space=pltpu.VMEM)
    hbm = pl.BlockSpec(memory_space=pl.ANY)
    own = jax.ShapeDtypeStruct((4, D), F32)
    own_b = jax.ShapeDtypeStruct((4, Q), F32)
    out = pl.pallas_call(
        functools.partial(kernel, ys, xs, zs, order),
        out_shape=(
            jax.ShapeDtypeStruct((Q, T), BF16),
            own,
            own_b,
            own,
            own,
            own_b,
            own_b,
            jax.ShapeDtypeStruct((ys, ms, RANK, D), BF16),
            jax.ShapeDtypeStruct((Q, c_rows), BF16),
        ),
        in_specs=[hbm] * 3 + [vmem] * 9,
        out_specs=(vmem,) * 7 + (hbm, vmem),
        scratch_shapes=shapes,
        compiler_params=pltpu.CompilerParams(
            collective_id=0, has_side_effects=True, vmem_limit_bytes=56 * 1024 * 1024
        ),
    )(tok, w, down, up.T, cot.T, idx.T, ma, mb, fa, sa, fb, sb)
    mixed, nma, nmb, nfa, nsa, nfb, nsb, reta, retb = out
    return (mixed.T, nma, nmb, nfa, nsa, nfb, nsb, reta.reshape(c_rows, D), retb.T)


def build(mesh, ys, xs, zs):
    both, width = P("dp", "fsdp"), P(None, "fsdp")
    return jax.shard_map(
        functools.partial(shards, ys, xs, zs),
        mesh=mesh,
        in_specs=(both, P("fsdp", None), width, width, both, P("dp", None)) + (both,) * 6,
        out_specs=(both,) * 7 + (width, width),
        check_vma=False,
    )


def solution(mesh):
    return build(mesh, YS, XS, ZS)
```

time: 454 us -> 78.3 us (0.17)
  blocking collectives: 348 us -> 0 us
  waiting for transfers between devices: 73.6 us -> 0 us
  Pallas kernels: 0 us -> 68.9 us
  between operations: 14.6 us -> 0.67 us
  matrix products: 8.41 us -> 0 us
    unnamed x1 -> x0, blocking collectives: 256 us -> none
    pallas_call x0 -> x1, Pallas kernels: none -> 68.9 us  [shards(): pl.pallas_call(functools.partial(kernel, ys, xs, zs, order), out_shape=(j...]
    all_gather x1 -> x0, blocking collectives: 55 us -> none  [shards(): lax.all_gather(new_master_b.astype(jnp.bfloat16), 'dp', axis=0, tiled=True)]
    psum x1 -> x0, waiting for transfers between devices: 41.3 us -> none  [shards(): lax.psum((base_part, rank_part, grad_part), 'fsdp')]
    psum x1 -> x0, blocking collectives: 36.6 us -> none  [shards(): lax.psum((base_part, rank_part, grad_part), 'fsdp')]
    all_gather x1 -> x0, waiting for transfers between devices: 32.3 us -> none  [shards(): lax.all_gather(new_master_a.astype(jnp.bfloat16), 'dp', axis=0, tiled=True)]
    dot_general x6 -> x0, matrix products: 8.41 us -> none  [the longest x1 2.03 us: shards(): lax.dot_general(grad_spread, tokens, (((0,), (0,)), ((), ())), preferred_...]
  transfers between devices with their start and end apart: 3 -> 0, of which waited for: 2 -> 0; matrix products, arithmetic and copies ran while one was open for 2% -> 0% of each run, Pallas kernels for 0% -> 0%
where the time goes in v1:
time: 78.3 us; the launch traced here: 77.9 us
  Pallas kernels  68.9 us (88%)
  local copies, waits for them, and re-layouts  8.31 us (11%)
    pallas_call x1, Pallas kernels, shards(): pl.pallas_call(functools.partial(kernel, ys, xs, zs, order), out_shape=(j...  68.9 us
    unnamed x23, local copies, waits for them, and re-layouts  8.31 us

profile of v1, /device:TPU:1, one launch (start us, length us, event | category | flops | bytes accessed | tf_op | source)
XLA Modules:
  0.0 77.9 jit_solution(5516039111504442227)
XLA Ops:
  0.6 68.9 %shard_map.187 = (bf16[64,512]{1,0:T(8,128)(2,1)}, f32[4,1024]{1,0:T(4,128)}, f32[4,64]{1,0:T(4,128)}, f32[4,1024]{1,0:T(4,128)}, f32[4,1024]{1,0:T(4,128)}, /*i...) custom-call(bf16[512,1024]{1,0:T(8,128)(2,1)} %refs_0_.1, ...), custom_call_target="tpu_custom_call" | custom-call | tf_op jit(solution)/shard_map/pallas_call | solution.py:524
  69.5 0.0 copy-start.3
  69.5 1.5 %copy.30 = bf16[512,64]{0,1:T(8,128)(2,1)} copy(bf16[512,64]{0,1:T(8,128)(2,1)} %bitcast.10) | data formatting | bytes 131072
  71.0 0.0 copy-done.3
  71.0 0.0 copy-start.6
  71.0 0.0 copy-start.2
  71.0 0.6 copy.31
  71.6 0.1 copy-done.6
  71.7 0.6 copy.32
  72.3 0.0 copy-done.2
  72.3 0.0 copy-start.1
  72.3 0.6 copy.33
  72.9 0.1 copy-done.1
  73.0 0.0 copy-start.5
  73.0 0.6 copy.34
  73.6 0.1 copy-done.5
  73.7 0.0 copy-start.4
  73.7 0.6 copy.35
  74.3 0.1 copy-done.4
  74.3 0.6 copy.36
  74.9 0.0 copy-start
  74.9 2.3 %copy.37 = bf16[512,1024]{1,0:T(8,128)(2,1)} copy(bf16[512,1024]{1,0:T(8,128)(2,1)} %bitcast.6) | data formatting | bytes 2097152
  77.2 0.0 copy-done
  77.2 0.6 copy.38
Async XLA Ops:
  69.5 1.5 %copy-start.3 = (f32[4,1024]{1,0:T(4,128)S(1)}, f32[4,1024]{1,0:T(4,128)}, u32[]{:S(2)}) copy-start(f32[4,1024]{1,0:T(4,128)} %get-tuple-element.37) | copy-start | bytes 49156
  71.0 0.7 copy-start.6
  71.0 1.3 %copy-start.2 = (f32[4,1024]{1,0:T(4,128)S(1)}, f32[4,1024]{1,0:T(4,128)}, u32[]{:S(2)}) copy-start(f32[4,1024]{1,0:T(4,128)} %get-tuple-element.39) | copy-start | bytes 49156
  72.3 0.7 copy-start.1
  73.0 0.7 copy-start.5
  73.7 0.7 copy-start.4
  74.9 2.3 %copy-start = (bf16[64,512]{1,0:T(8,128)(2,1)S(1)}, bf16[64,512]{1,0:T(8,128)(2,1)}, u32[]{:S(2)}) copy-start(bf16[64,512]{1,0:T(8,128)(2,1)} %get-tuple-element.26) | copy-start | bytes 196612

commit v2 on v1

--- a/solution.py
+++ b/solution.py
@@ -1,4 +1,5 @@
 import functools
+from itertools import zip_longest
 
 import jax
 import jax.numpy as jnp
@@ -50,6 +51,15 @@
         tok=v((T, D), BF16),
         down=v((c, D), BF16),
         w=v((D, zs * Q), BF16),
+        up=v((Q, c), BF16),
+        cot=v((Q, T), BF16),
+        idx=v((1, T), jnp.int32),
+        ma=v((4, D), F32),
+        fa_=v((4, D), F32),
+        sa=v((4, D), F32),
+        mb=v((4, Q), F32),
+        fb_=v((4, Q), F32),
+        sb=v((4, Q), F32),
         proj=v((c, T), F32),
         spread_r=v((c, T), BF16),
         spread_g=v((c, T), BF16),
@@ -78,26 +88,29 @@
         a1r=v((xs, ys, RANK, LANES), BF16),
         a2x=v((ys, RANK, LANES), F32),
         a2r=v((ys, RANK, LANES), F32),
-        b1x=v((ys, xs + nb, RANK, LANES), BF16),
-        b1r=v((ys, xs + nb, RANK, LANES), BF16),
-        b2x=v((xs, 2, RANK, LANES), F32),
-        b2r=v((xs, 2, RANK, LANES), F32),
+        b1x=v((ys, xs, RANK, LANES), BF16),
+        b1r=v((ys, xs, RANK, LANES), BF16),
+        b2x=v((xs, RANK, LANES), F32),
+        b2r=v((xs, RANK, LANES), F32),
+        u1x=v((ys, nb, RANK, LANES), BF16),
+        u1r=v((ys, nb, RANK, LANES), BF16),
+        u2x=v((nb, RANK, LANES), F32),
+        u2r=v((xs, RANK, LANES), F32),
         g4=v((4, 4, 256), F32),
         g4r=v((4, 4, 256), F32),
         bq=v((4, 4, Q), F32),
-        tile_b=v((RANK, LANES), BF16),
-        rows=v((ys, ms, RANK, D), BF16),
         bg=v((xs, RANK, LANES), BF16),
         bt=v((ys, nb, RANK, LANES), BF16),
         bs=v((ys, nb, RANK, LANES), BF16),
         ball=v((c, LANES), F32),
     )
     sems = dict(
-        load=3, gz1=zs, gz2=zs, rz1=zs, rz2=zs, bz=zs, cc=1, cx=xs, cy=ys, pf=4, sib=3,
-        a1=xs, b1=ys, a2=ys, b2=xs, ret=4, ay=ys, ax=xs, bx_=xs, by=ys, bbx=xs, bby=ys, bbs=1,
-        fa=xs, fb=ys, out=1,
-    )
-    local = ("load", "out")
+        load=12, gz1=zs, gz2=zs, rz1=zs, rz2=zs, bz=zs, cc=1, cx=xs, cy=ys, pf=4, sib=3,
+        a1=2 * xs, b1=2 * ys, a2=ys, b2=xs, u1=ys, u2=xs, ret=4, ay=ys, ax=xs * (ys // 2),
+        bx_=xs, by=ys * ms, bbx=xs, bby=ys, bbs=1,
+        fa=xs, fb=ys,
+    )
+    local = ("load",)
     order = list(bufs)
     shapes = list(bufs.values())
     for name, n in sems.items():
@@ -109,7 +122,8 @@
     return order, shapes
 
 
-INPUTS = ("tok_h", "w_h", "down_h", "up", "cot", "idx", "ma", "mb", "fa_", "sa", "fb_", "sb")
+INPUTS = ("tok", "w", "down", "up", "cot", "idx", "ma", "mb", "fa_", "sa", "fb_", "sb")
+LOADS = ("up", "cot", "idx", "down", "tok", "w", "ma", "fa_", "sa", "mb", "fb_", "sb")
 OUTPUTS = ("mixed", "nma", "nmb", "nfa", "nsa", "nfb", "nsb", "reta", "retb")
 
 
@@ -119,7 +133,8 @@
 
 
 def kernel(ys, xs, zs, order, *refs):
-    r = Refs(INPUTS + OUTPUTS + tuple(order), refs)
+    hbm = dict(zip(INPUTS, refs))
+    r = Refs(OUTPUTS + tuple(order), refs[len(INPUTS) :])
     ms = xs // 2
     nb = ms // 2
     na = ys * ms
@@ -173,12 +188,11 @@
     sibling = at(cc=1 - core)
     kx, ky, kz = far_first(xs), far_first(ys), far_first(zs)
 
-    load_tok = pltpu.make_async_copy(r.tok_h, r.tok, r.load_s.at[0])
-    load_down = pltpu.make_async_copy(r.down_h, r.down, r.load_s.at[1])
-    load_w = pltpu.make_async_copy(r.w_h, r.w, r.load_s.at[2])
-    load_down.start()
-    load_tok.start()
-    load_w.start()
+    loads = {}
+    for i, name in enumerate(LOADS):
+        loads[name] = pltpu.make_async_copy(hbm[name], getattr(r, name), r.load_s.at[i])
+        if i < 3:
+            loads[name].start()
 
     barrier = pltpu.get_barrier_semaphore()
     partners = [at(zz=zp(k)) for k in kz] + [at(xx=xp(k)) for k in kx] + [at(yy=yp(k)) for k in ky]
@@ -187,6 +201,10 @@
     for device in partners:
         pl.semaphore_signal(barrier, inc=1, device_id=device, device_id_type=MESH)
 
+    for name in LOADS[3:]:
+        loads[name].start()
+    for name in ("up", "cot", "idx"):
+        loads[name].wait()
     idx = r.idx[...]
     idx16 = jnp.broadcast_to(idx, (RANK, T))
 
@@ -221,23 +239,56 @@
         r.up[...], r.cot[...], (((0,), (0,)), ((), ())), preferred_element_type=F32
     )
     to_blocks(chosen(r.proj), r.gx)
+    pl.semaphore_wait(barrier, len(partners))
+
+    gz1 = [(k, send(r.gx.at[zp(k)], r.gr.at[k], "gz1", k, at(zz=zp(k)))) for k in kz]
     ids = lax.broadcasted_iota(jnp.int32, (LANES, T), 0)
     onehot = jnp.where(ids == jnp.broadcast_to(idx, (LANES, T)), 1.0, 0.0).astype(BF16)
     counts = lax.dot_general(
         jnp.ones((8, T), BF16), onehot, (((1,), (1,)), ((), ())), preferred_element_type=F32
     )
     r.c0[...] = counts
+    cc = send(r.c0, r.c0r, "cc", 0, sibling)
+    loads["down"].wait()
+    loads["tok"].wait()
+    r.proj[...] = lax.dot_general(
+        r.down[...], r.tok[...], (((1,), (1,)), ((), ())), preferred_element_type=F32
+    )
+    to_blocks(chosen(r.proj), r.rx)
+    rz1 = [(k, send(r.rx.at[zp(k)], r.rr.at[k], "rz1", k, at(zz=zp(k)))) for k in kz]
+
+    total = r.gx[z]
+    for k, copy in gz1:
+        copy.wait_recv()
+        total = total + r.gr[k]
+    r.gg[z] = (0.25 * total).astype(BF16).astype(F32)
+    gz2 = [(k, send(r.gg.at[z], r.gg.at[z], "gz2", k, at(zz=zp(k)))) for k in kz]
+
+    loads["w"].wait()
+    lane = lax.broadcasted_iota(jnp.int32, (T // 2, LANES), 1)
+    for i in range(zs // 2):
+        part = jnp.dot(
+            r.tok[...], r.w[:, i * LANES : (i + 1) * LANES], preferred_element_type=F32
+        )
+        top, bottom = part[: T // 2], part[T // 2 :]
+        r.bx[2 * i] = jnp.where(lane < Q, top, pltpu.roll(bottom, Q, 1)).astype(BF16)
+        r.bx[2 * i + 1] = jnp.where(lane < Q, pltpu.roll(top, Q, 1), bottom).astype(BF16)
+
+    total = r.rx[z]
+    for k, copy in rz1:
+        copy.wait_recv()
+        total = total + r.rr[k]
+    r.rg[z] = (SCALE * total).astype(BF16).astype(F32)
+    rz2 = [(k, send(r.rg.at[z], r.rg.at[z], "rz2", k, at(zz=zp(k)))) for k in kz]
+
+    for name in ("ma", "fa_", "sa", "mb", "fb_", "sb"):
+        loads[name].wait()
     for j in range(4):
         hj, cj = j // 2, j % 2
         for i, ref in enumerate((r.ma, r.fa_, r.sa)):
             col = cj * (D // 2) + hj * LANES
             r.pfx[j, i, :, 0:LANES] = ref[:, col : col + LANES]
             r.pfx[j, i, :, LANES : 2 * LANES] = ref[:, col + 256 : col + 256 + LANES]
-
-    pl.semaphore_wait(barrier, len(partners))
-
-    gz1 = [(k, send(r.gx.at[zp(k)], r.gr.at[k], "gz1", k, at(zz=zp(k)))) for k in kz]
-    cc = send(r.c0, r.c0r, "cc", 0, sibling)
     pf = []
     for k in range(1, 4):
         hk, ck = k // 2, k % 2
@@ -249,38 +300,6 @@
             )
         )
 
-    load_down.wait()
-    load_tok.wait()
-    r.proj[...] = lax.dot_general(
-        r.down[...], r.tok[...], (((1,), (1,)), ((), ())), preferred_element_type=F32
-    )
-    to_blocks(chosen(r.proj), r.rx)
-    rz1 = [(k, send(r.rx.at[zp(k)], r.rr.at[k], "rz1", k, at(zz=zp(k)))) for k in kz]
-
-    total = r.gx[z]
-    for k, copy in gz1:
-        copy.wait_recv()
-        total = total + r.gr[k]
-    r.gg[z] = (0.25 * total).astype(BF16).astype(F32)
-    gz2 = [(k, send(r.gg.at[z], r.gg.at[z], "gz2", k, at(zz=zp(k)))) for k in kz]
-
-    load_w.wait()
-    lane = lax.broadcasted_iota(jnp.int32, (T // 2, LANES), 1)
-    for i in range(zs // 2):
-        part = jnp.dot(
-            r.tok[...], r.w[:, i * LANES : (i + 1) * LANES], preferred_element_type=F32
-        )
-        top, bottom = part[: T // 2], part[T // 2 :]
-        r.bx[2 * i] = jnp.where(lane < Q, top, pltpu.roll(bottom, Q, 1)).astype(BF16)
-        r.bx[2 * i + 1] = jnp.where(lane < Q, pltpu.roll(top, Q, 1), bottom).astype(BF16)
-
-    total = r.rx[z]
-    for k, copy in rz1:
-        copy.wait_recv()
-        total = total + r.rr[k]
-    r.rg[z] = (SCALE * total).astype(BF16).astype(F32)
-    rz2 = [(k, send(r.rg.at[z], r.rg.at[z], "rz2", k, at(zz=zp(k)))) for k in kz]
-
     for _, copy in gz2:
         copy.wait_recv()
     spread_into(from_blocks(r.gg), r.spread_g)
@@ -293,16 +312,32 @@
         columns = pl.ds(pl.multiple_of(half + part * 256, 256), 256)
         r.own[part] = jnp.dot(r.spread_g[...], r.tok[:, columns], preferred_element_type=F32)
 
-    def chip_sum(part, a, hh):
-        rows = slice(a * RANK, (a + 1) * RANK)
-        cols = slice(hh * LANES, (hh + 1) * LANES)
+    def chip_sum(part, yy, xx):
+        rows = pl.ds(pl.multiple_of((yy * ms + xx // 2) * RANK, RANK), RANK)
+        cols = pl.ds(pl.multiple_of((xx % 2) * LANES, LANES), LANES)
         return (r.own[part, rows, cols] + r.sr[part, rows, cols]).astype(BF16)
 
+    oy, ox = ky + [0], kx + [0]
+    cuts_y = (slice(0, max(1, 3 * ys // 8)), slice(max(1, 3 * ys // 8), ys))
+    cuts_x = (slice(0, max(1, 3 * xs // 8)), slice(max(1, 3 * xs // 8), xs))
     sib[0].wait_recv()
-    for xx in range(xs):
-        for yy in range(ys):
-            r.a1x[xx, yy] = chip_sum(0, yy * ms + xx // 2, xx % 2)
-    a1 = [(k, send(r.a1x.at[xp(k)], r.a1r.at[k], "a1", k, at(xx=xp(k)))) for k in kx]
+    a1 = []
+    for g, group in enumerate(cuts_y):
+        for i in range(group.start, group.stop):
+            for xx in range(xs):
+                r.a1x[xx, i] = chip_sum(0, yp(oy[i]), xx)
+        for k in kx:
+            src, dst = r.a1x.at[xp(k), group], r.a1r.at[k, group]
+            a1.append(send(src, dst, "a1", g * xs + k, at(xx=xp(k))))
+    sib[1].wait_recv()
+    b1 = []
+    for g, group in enumerate(cuts_x):
+        for i in range(group.start, group.stop):
+            for yy in range(ys):
+                r.b1x[yy, i] = chip_sum(1, yy, xp(ox[i]))
+        for k in ky:
+            src, dst = r.b1x.at[yp(k), group], r.b1r.at[k, group]
+            b1.append(send(src, dst, "b1", g * ys + k, at(yy=yp(k))))
 
     for _, copy in rz2:
         copy.wait_recv()
@@ -320,21 +355,17 @@
             )
     sib.append(send(r.sbx, r.sbr, "sib", 2, sibling))
 
-    sib[1].wait_recv()
-    for yy in range(ys):
-        for xx in range(xs):
-            r.b1x[yy, xx] = chip_sum(1, yy * ms + xx // 2, xx % 2)
+    cc.wait_recv()
+    r.c1[...] = r.c0[...] + r.c0r[...]
+    cx = [(k, send(r.c1, r.c1r.at[k], "cx", k, at(xx=xp(k)))) for k in kx]
     sib[2].wait_recv()
     for yy in range(ys):
         for s in range(nb):
-            r.b1x[yy, xs + s] = (r.sbx[yy, s] + r.sbr[yy, s]).astype(BF16)
-    b1 = [(k, send(r.b1x.at[yp(k)], r.b1r.at[k], "b1", k, at(yy=yp(k)))) for k in ky]
+            r.u1x[yy, s] = (r.sbx[yy, s] + r.sbr[yy, s]).astype(BF16)
+    u1 = [(k, send(r.u1x.at[yp(k)], r.u1r.at[k], "u1", k, at(yy=yp(k)))) for k in ky]
 
     base = [(k, send(r.bx.at[zp(k)], r.br.at[k], "bz", k, at(zz=zp(k)))) for k in kz]
 
-    cc.wait_recv()
-    r.c1[...] = r.c0[...] + r.c0r[...]
-    cx = [(k, send(r.c1, r.c1r.at[k], "cx", k, at(xx=xp(k)))) for k in kx]
     total = r.c1[...]
     for k, copy in cx:
         copy.wait_recv()
@@ -342,26 +373,36 @@
     r.c2[...] = total
     cy = [(k, send(r.c2, r.c2r.at[k], "cy", k, at(yy=yp(k)))) for k in ky]
 
-    for _, copy in a1:
-        copy.wait_recv()
-    for yy in range(ys):
-        total = r.a1x[x, yy].astype(F32)
-        for k in kx:
-            total = total + r.a1r[k, yy].astype(F32)
-        r.a2x[yy] = total
-    a2 = [(k, send(r.a2x.at[yp(k)], r.a2r.at[k], "a2", k, at(yy=yp(k)))) for k in ky]
-    for _, copy in b1:
-        copy.wait_recv()
-    sums = []
-    for s in range(xs + nb):
-        total = r.b1x[y, s].astype(F32)
+    a2, b2 = [], []
+    for g in range(2):
+        for copy in a1[g * len(kx) : (g + 1) * len(kx)]:
+            copy.wait_recv()
+        for i in range(cuts_y[g].start, cuts_y[g].stop):
+            total = r.a1x[x, i].astype(F32)
+            for k in kx:
+                total = total + r.a1r[k, i].astype(F32)
+            r.a2x[i] = total
+            k = oy[i]
+            if k:
+                a2.append((k, send(r.a2x.at[i], r.a2r.at[k], "a2", k, at(yy=yp(k)))))
+        for copy in b1[g * len(ky) : (g + 1) * len(ky)]:
+            copy.wait_recv()
+        for i in range(cuts_x[g].start, cuts_x[g].stop):
+            total = r.b1x[y, i].astype(F32)
+            for k in ky:
+                total = total + r.b1r[k, i].astype(F32)
+            r.b2x[i] = total
+            k = ox[i]
+            if k:
+                b2.append((k, send(r.b2x.at[i], r.b2r.at[k], "b2", k, at(xx=xp(k)))))
+    for _, copy in u1:
+        copy.wait_recv()
+    for s in range(nb):
+        total = r.u1x[y, s].astype(F32)
         for k in ky:
-            total = total + r.b1r[k, s].astype(F32)
-        sums.append(total)
-    for xx in range(xs):
-        r.b2x[xx, 0] = sums[xx]
-        r.b2x[xx, 1] = sums[xs + xx // 4]
-    b2 = [(k, send(r.b2x.at[xp(k)], r.b2r.at[k], "b2", k, at(xx=xp(k)))) for k in kx]
+            total = total + r.u1r[k, s].astype(F32)
+        r.u2x[s] = total
+    u2 = [(k, send(r.u2x.at[xp(k) // 4], r.u2r.at[k], "u2", k, at(xx=xp(k)))) for k in kx]
 
     total = r.c2[...]
     for k, copy in cy:
@@ -384,31 +425,33 @@
             r.g4[j, :, part * LANES : (part + 1) * LANES] = gradient[4 * j : 4 * j + 4]
         new_master, _, _ = adam_step(unit(0, part), unit(1, part), unit(2, part), gradient)
         columns = pl.ds(pl.multiple_of(half + part * 256 + h * LANES, LANES), LANES)
-        r.rows[y, m, :, columns] = new_master.astype(BF16)
+        r.reta[y, m, :, columns] = new_master.astype(BF16)
 
     cols_a = pl.ds(pl.multiple_of(half + h * LANES, LANES), LANES)
     cols_b = pl.ds(pl.multiple_of(half + 256 + h * LANES, LANES), LANES)
     wide_b = pl.ds(pl.multiple_of(half + 256, 256), 256)
 
-    total = r.a2x[y]
+    total = r.a2x[ys - 1]
     for k, copy in a2:
         copy.wait_recv()
         total = total + r.a2r[k]
     update_unit(0, total)
-    tile = r.rows.at[y, m, :, cols_a]
+    tile = r.reta.at[y, m, :, cols_a]
     ay = [(k, send(tile, tile, "ay", k, at(yy=yp(k)))) for k in ky]
 
-    total = r.b2x[x, 0]
-    total_b = r.b2x[x, 1]
+    total = r.b2x[xs - 1]
     for k, copy in b2:
         copy.wait_recv()
-        total = total + r.b2r[k, 0]
-        total_b = total_b + r.b2r[k, 1]
+        total = total + r.b2r[k]
     update_unit(1, total)
-    tile = r.rows.at[y, m, :, cols_b]
+    tile = r.reta.at[y, m, :, cols_b]
     bx_ = [(k, send(tile, tile, "bx_", k, at(xx=xp(k)))) for k in kx]
 
     odd = m % 2
+    total_b = r.u2x[x // 4]
+    for k, copy in u2:
+        copy.wait_recv()
+        total_b = total_b + r.u2r[k]
     for j in range(4):
         r.bq[j] = jnp.where(
             odd == 1, total_b[4 * j : 4 * j + 4, Q:], total_b[4 * j : 4 * j + 4, :Q]
@@ -433,15 +476,40 @@
             send(r.g4.at[2 * h2 + c2], r.g4r.at[q], "ret", k, at(xx=2 * m + h2, cc=c2))
         )
 
-    for _, copy in ay:
-        copy.wait_recv()
-    column_a = r.rows.at[:, m, :, cols_a]
-    ax = [(k, send(column_a, column_a, "ax", k, at(xx=xp(k)))) for k in kx]
+    def pairs(me, count):
+        step = 2 * (me % 2) - 1
+        offsets = {4: (0, step, -step, 2), 2: (0, 1), 1: (0,)}[count]
+        return [lax.rem(me // 2 + o + count, count) for o in offsets]
+
+    def arrived(name, tile, me, source, n, device):
+        slot = lax.rem(me - source + n, n)
+        pltpu.make_async_remote_copy(
+            src_ref=tile,
+            dst_ref=tile,
+            send_sem=getattr(r, name + "_s").at[slot],
+            recv_sem=getattr(r, name + "_r").at[slot],
+            device_id=device,
+            device_id_type=MESH,
+        ).wait_recv()
+
+    column_a = r.reta.at[:, m, :, cols_a]
+    row_b = r.reta.at[y, :, :, wide_b]
+    tile_a, tile_b = r.reta.at[y, m, :, cols_a], r.reta.at[y, m, :, cols_b]
+    ax, by = [], []
+    for j, (pa, pb) in enumerate(zip_longest(pairs(y, ys // 2), pairs(x, ms))):
+        if pa is not None:
+            for source in [2 * pa, 2 * pa + 1] if j else [2 * pa + 1 - y % 2]:
+                arrived("ay", tile_a, y, source, ys, at(yy=source))
+            region = r.reta.at[pl.ds(2 * pa, 2), m, :, cols_a]
+            for k in kx:
+                ax.append((k, send(region, region, "ax", j * xs + k, at(xx=xp(k)))))
+        if pb is not None:
+            for source in [2 * pb, 2 * pb + 1] if j else [2 * pb + 1 - x % 2]:
+                arrived("bx_", tile_b, x, source, xs, at(xx=source))
+            region = r.reta.at[y, pb, :, wide_b]
+            for k in ky:
+                by.append((k, send(region, region, "by", j * ys + k, at(yy=yp(k)))))
     fa = [send(column_a, column_a, "fa", 0, sibling)]
-    for _, copy in bx_:
-        copy.wait_recv()
-    row_b = r.rows.at[y, :, :, wide_b]
-    by = [(k, send(row_b, row_b, "by", k, at(yy=yp(k)))) for k in ky]
     fb = [send(row_b, row_b, "fb", 0, sibling)]
     for _, copy in bbx:
         copy.wait_recv()
@@ -479,27 +547,29 @@
     r.mixed[:, : T // 2] = (turned[:Q] + 0.25 * term[:, : T // 2]).astype(BF16)
     r.mixed[:, T // 2 :] = (turned[Q:] + 0.25 * term[:, T // 2 :]).astype(BF16)
 
-    for k, copy in ax:
-        copy.wait_recv()
+    for k in kx:
+        for other, copy in ax:
+            if other == k:
+                copy.wait_recv()
         source = from_x(k)
-        region = r.rows.at[
+        region = r.reta.at[
             :,
             source // 2,
             :,
             pl.ds(pl.multiple_of(half + (source % 2) * LANES, LANES), LANES),
         ]
         fa.append(send(region, region, "fa", k, sibling))
-    for k, copy in by:
-        copy.wait_recv()
-        region = r.rows.at[from_y(k), :, :, wide_b]
+    for k in ky:
+        for other, copy in by:
+            if other == k:
+                copy.wait_recv()
+        region = r.reta.at[from_y(k), :, :, wide_b]
         fb.append(send(region, region, "fb", k, sibling))
     for _, copy in bby:
         copy.wait_recv()
     bbs = send(r.bt, r.bs, "bbs", 0, sibling)
     for copy in fa + fb:
         copy.wait_recv()
-    out = pltpu.make_async_copy(r.rows, r.reta, r.out_s.at[0])
-    out.start()
     bbs.wait_recv()
     for yy in range(ys):
         for s in range(nb):
@@ -508,9 +578,17 @@
             r.ball[row : row + RANK, :] = both
             r.ball[row + RANK : row + 2 * RANK, :] = pltpu.roll(both, Q, 1)
     r.retb[...] = jnp.transpose(r.ball[...])[:Q].astype(BF16)
-    out.wait()
     for copy in started:
         copy.wait_send()
+
+
+def place(*refs):
+    sems = refs[18]
+    copies = [pltpu.make_async_copy(refs[i], refs[9 + i], sems.at[i]) for i in range(9)]
+    for copy in copies:
+        copy.start()
+    for copy in copies:
+        copy.wait()
 
 
 def shards(ys, xs, zs, tok, w, down, up, cot, idx, ma, mb, fa, sa, fb, sb):
@@ -519,28 +597,28 @@
     order, shapes = scratch(ys, xs, zs)
     vmem = pl.BlockSpec(memory_space=pltpu.VMEM)
     hbm = pl.BlockSpec(memory_space=pl.ANY)
-    own = jax.ShapeDtypeStruct((4, D), F32)
-    own_b = jax.ShapeDtypeStruct((4, Q), F32)
+    own, own_b = ((4, D), F32), ((4, Q), F32)
+    results = (
+        ((Q, T), BF16), own, own_b, own, own, own_b, own_b,
+        ((ys, ms, RANK, D), BF16), ((Q, c_rows), BF16),
+    )
     out = pl.pallas_call(
         functools.partial(kernel, ys, xs, zs, order),
-        out_shape=(
-            jax.ShapeDtypeStruct((Q, T), BF16),
-            own,
-            own_b,
-            own,
-            own,
-            own_b,
-            own_b,
-            jax.ShapeDtypeStruct((ys, ms, RANK, D), BF16),
-            jax.ShapeDtypeStruct((Q, c_rows), BF16),
-        ),
-        in_specs=[hbm] * 3 + [vmem] * 9,
-        out_specs=(vmem,) * 7 + (hbm, vmem),
+        out_shape=tuple(pltpu.VMEM(shape, dtype) for shape, dtype in results),
+        in_specs=[hbm] * 12,
+        out_specs=(vmem,) * 9,
         scratch_shapes=shapes,
         compiler_params=pltpu.CompilerParams(
             collective_id=0, has_side_effects=True, vmem_limit_bytes=56 * 1024 * 1024
         ),
     )(tok, w, down, up.T, cot.T, idx.T, ma, mb, fa, sa, fb, sb)
+    out = pl.pallas_call(
+        place,
+        out_shape=tuple(jax.ShapeDtypeStruct(shape, dtype) for shape, dtype in results),
+        in_specs=[vmem] * 9,
+        out_specs=(hbm,) * 9,
+        scratch_shapes=[pltpu.SemaphoreType.DMA((9,))],
+    )(*(pltpu.with_memory_space_constraint(o, pltpu.VMEM) for o in out))
     mixed, nma, nmb, nfa, nsa, nfb, nsb, reta, retb = out
     return (mixed.T, nma, nmb, nfa, nsa, nfb, nsb, reta.reshape(c_rows, D), retb.T)
 

time: 78.3 us -> 69.9 us (0.89)
  local copies, waits for them, and re-layouts: 8.31 us -> 0 us
    unnamed x23 -> x0, local copies, waits for them, and re-layouts: 8.31 us -> none
    pallas_call x1 -> x2, Pallas kernels: 68.9 us -> 69.1 us  [the longest x1 67.9 us: shards(): pl.pallas_call(functools.partial(kernel, ys, xs, zs, order), out_shape=tu...]
where the time goes in v2:
time: 69.9 us; the launch traced here: 69.7 us
  Pallas kernels  69.1 us (99%)
    pallas_call x1, Pallas kernels, shards(): pl.pallas_call(functools.partial(kernel, ys, xs, zs, order), out_shape=tu...  67.9 us

profile of v2, /device:TPU:1, one launch (start us, length us, event | category | flops | bytes accessed | tf_op | source)
XLA Modules:
  0.0 69.7 jit_solution(1575406738450195400)
XLA Ops:
  0.6 67.9 %shard_map.187 = (bf16[64,512]{1,0:T(8,128)(2,1)S(1)}, f32[4,1024]{1,0:T(4,128)S(1)}, f32[4,64]{1,0:T(4,128)S(1)}, f32[4,1024]{1,0:T(4,128)S(1)}, f32[4,1024]{1,...) custom-call(bf16[512,1024]{1,0:T(8,128)(2,1)} %refs_0_.1, ...), custom_call_target="tpu_custom_call" | custom-call | tf_op jit(solution)/shard_map/pallas_call | solution.py:605
  68.6 1.1 %shard_map.188 = (bf16[64,512]{1,0:T(8,128)(2,1)}, f32[4,1024]{1,0:T(4,128)}, f32[4,64]{1,0:T(4,128)}, f32[4,1024]{1,0:T(4,128)}, f32[4,1024]{1,0:T(4,128)}, /*i...) custom-call(bf16[64,512]{1,0:T(8,128)(2,1)S(1)} %get-tuple-element.27.refs_0_, ...), custom_call_target="tpu_custom_call" | custom-call | tf_op jit(solution)/shard_map/pallas_call | solution.py:615

commit v3 on v2

--- a/solution.py
+++ b/solution.py
@@ -17,6 +17,8 @@
 ADAM_EPS = 1e-08
 LEARN_RATE = 0.01
 SCALE = 1.0 / MODEL_WIDTH**0.5
+
+SUM_PARTS, GATHER_PARTS = 2, 2
 
 MESH = pl.DeviceIdType.MESH
 F32 = jnp.float32
@@ -95,19 +97,19 @@
         u1x=v((ys, nb, RANK, LANES), BF16),
         u1r=v((ys, nb, RANK, LANES), BF16),
         u2x=v((nb, RANK, LANES), F32),
-        u2r=v((xs, RANK, LANES), F32),
+        u2r=v((xs, nb, RANK, LANES), F32),
+        ug=v((nb, RANK, LANES), F32),
+        pm=v((2, xs, 3, 4, Q), F32),
         g4=v((4, 4, 256), F32),
         g4r=v((4, 4, 256), F32),
         bq=v((4, 4, Q), F32),
-        bg=v((xs, RANK, LANES), BF16),
         bt=v((ys, nb, RANK, LANES), BF16),
-        bs=v((ys, nb, RANK, LANES), BF16),
         ball=v((c, LANES), F32),
     )
     sems = dict(
         load=12, gz1=zs, gz2=zs, rz1=zs, rz2=zs, bz=zs, cc=1, cx=xs, cy=ys, pf=4, sib=3,
         a1=2 * xs, b1=2 * ys, a2=ys, b2=xs, u1=ys, u2=xs, ret=4, ay=ys, ax=xs * (ys // 2),
-        bx_=xs, by=ys * ms, bbx=xs, bby=ys, bbs=1,
+        bx_=xs, by=ys * ms, pm=xs, pms=1, bby=ys,
         fa=xs, fb=ys,
     )
     local = ("load",)
@@ -289,6 +291,10 @@
             col = cj * (D // 2) + hj * LANES
             r.pfx[j, i, :, 0:LANES] = ref[:, col : col + LANES]
             r.pfx[j, i, :, LANES : 2 * LANES] = ref[:, col + 256 : col + 256 + LANES]
+    for i, ref in enumerate((r.mb, r.fb_, r.sb)):
+        r.pm[core, x, i] = ref[...]
+    mine = r.pm.at[core, x]
+    pm = [send(mine, mine, "pm", k, at(xx=xp(k))) for k in kx]
     pf = []
     for k in range(1, 4):
         hk, ck = k // 2, k % 2
@@ -320,6 +326,8 @@
     oy, ox = ky + [0], kx + [0]
     cuts_y = (slice(0, max(1, 3 * ys // 8)), slice(max(1, 3 * ys // 8), ys))
     cuts_x = (slice(0, max(1, 3 * xs // 8)), slice(max(1, 3 * xs // 8), xs))
+    if SUM_PARTS == 1:
+        cuts_y, cuts_x = (slice(0, ys),), (slice(0, xs),)
     sib[0].wait_recv()
     a1 = []
     for g, group in enumerate(cuts_y):
@@ -364,6 +372,10 @@
             r.u1x[yy, s] = (r.sbx[yy, s] + r.sbr[yy, s]).astype(BF16)
     u1 = [(k, send(r.u1x.at[yp(k)], r.u1r.at[k], "u1", k, at(yy=yp(k)))) for k in ky]
 
+    for copy in pm:
+        copy.wait_recv()
+    pms = send(r.pm.at[core], r.pm.at[core], "pms", 0, sibling)
+
     base = [(k, send(r.bx.at[zp(k)], r.br.at[k], "bz", k, at(zz=zp(k)))) for k in kz]
 
     total = r.c1[...]
@@ -374,7 +386,7 @@
     cy = [(k, send(r.c2, r.c2r.at[k], "cy", k, at(yy=yp(k)))) for k in ky]
 
     a2, b2 = [], []
-    for g in range(2):
+    for g in range(SUM_PARTS):
         for copy in a1[g * len(kx) : (g + 1) * len(kx)]:
             copy.wait_recv()
         for i in range(cuts_y[g].start, cuts_y[g].stop):
@@ -402,15 +414,30 @@
         for k in ky:
             total = total + r.u1r[k, s].astype(F32)
         r.u2x[s] = total
-    u2 = [(k, send(r.u2x.at[xp(k) // 4], r.u2r.at[k], "u2", k, at(xx=xp(k)))) for k in kx]
+    u2 = [(k, send(r.u2x, r.u2r.at[k], "u2", k, at(xx=xp(k)))) for k in kx]
 
     total = r.c2[...]
     for k, copy in cy:
         copy.wait_recv()
         total = total + r.c2r[k]
     lane8 = lax.broadcasted_iota(jnp.int32, (8, LANES), 1)
-    count = jnp.sum(jnp.where(lane8 == y * ms + m, total, 0.0), axis=1, keepdims=True)
-    count16 = jnp.concatenate([jnp.broadcast_to(count, (8, LANES))] * 2, axis=0)
+
+    def count_of(adapter):
+        count = jnp.sum(jnp.where(lane8 == y * ms + adapter, total, 0.0), axis=1, keepdims=True)
+        return jnp.concatenate([jnp.broadcast_to(count, (8, LANES))] * 2, axis=0)
+
+    count16 = count_of(m)
+    count_b = [jnp.where(lane16 < Q, count_of(2 * s), count_of(2 * s + 1)) for s in range(nb)]
+    pms.wait_recv()
+
+    def side_by_side(i, s):
+        halves = []
+        for adapter in (2 * s, 2 * s + 1):
+            rows = [r.pm[j % 2, 2 * adapter + j // 2, i] for j in range(4)]
+            halves.append(jnp.concatenate(rows, axis=0))
+        return jnp.concatenate(halves, axis=1)
+
+    states_b = [[side_by_side(i, s) for i in range(3)] for s in range(nb)]
     r.pfr[q] = r.pfx[q]
     for copy in pf:
         copy.wait_recv()
@@ -447,25 +474,25 @@
     tile = r.reta.at[y, m, :, cols_b]
     bx_ = [(k, send(tile, tile, "bx_", k, at(xx=xp(k)))) for k in kx]
 
+    sums_b = [r.u2x[s] for s in range(nb)]
+    for k, copy in u2:
+        copy.wait_recv()
+        for s in range(nb):
+            sums_b[s] = sums_b[s] + r.u2r[k, s]
+    for s in range(nb):
+        gradient = 0.25 * sums_b[s] / count_b[s]
+        r.ug[s] = gradient
+        r.bt[y, s] = adam_step(*states_b[s], gradient)[0].astype(BF16)
+    bby = [(k, send(r.bt.at[y], r.bt.at[y], "bby", k, at(yy=yp(k)))) for k in ky]
+
     odd = m % 2
-    total_b = r.u2x[x // 4]
-    for k, copy in u2:
-        copy.wait_recv()
-        total_b = total_b + r.u2r[k]
+    own_b = r.ug[x // 4]
     for j in range(4):
-        r.bq[j] = jnp.where(
-            odd == 1, total_b[4 * j : 4 * j + 4, Q:], total_b[4 * j : 4 * j + 4, :Q]
-        )
-    gradient = 0.25 * r.bq[q] / count16[:4, :Q]
-    new_master, new_first, new_second = adam_step(r.mb[...], r.fb_[...], r.sb[...], gradient)
+        r.bq[j] = jnp.where(odd == 1, own_b[4 * j : 4 * j + 4, Q:], own_b[4 * j : 4 * j + 4, :Q])
+    new_master, new_first, new_second = adam_step(r.mb[...], r.fb_[...], r.sb[...], r.bq[q])
     r.nmb[...] = new_master
     r.nfb[...] = new_first
     r.nsb[...] = new_second
-    wide = jnp.concatenate([new_master, new_master], axis=1)
-    lane4 = lax.broadcasted_iota(jnp.int32, (4, LANES), 1)
-    wide = jnp.where((lane4 // Q) == odd, wide, 0.0)
-    r.bg[x] = jnp.concatenate([jnp.where(q == j, wide, 0.0) for j in range(4)], axis=0).astype(BF16)
-    bbx = [(k, send(r.bg.at[x], r.bg.at[x], "bbx", k, at(xx=xp(k)))) for k in kx]
 
     ret = []
     for k in range(1, 4):
@@ -476,10 +503,11 @@
             send(r.g4.at[2 * h2 + c2], r.g4r.at[q], "ret", k, at(xx=2 * m + h2, cc=c2))
         )
 
-    def pairs(me, count):
+    def parts_of(me, n):
+        count = min(GATHER_PARTS, n // 2)
         step = 2 * (me % 2) - 1
         offsets = {4: (0, step, -step, 2), 2: (0, 1), 1: (0,)}[count]
-        return [lax.rem(me // 2 + o + count, count) for o in offsets]
+        return count, n // count, [lax.rem(me // (n // count) + o + count, count) for o in offsets]
 
     def arrived(name, tile, me, source, n, device):
         slot = lax.rem(me - source + n, n)
@@ -492,34 +520,32 @@
             device_id_type=MESH,
         ).wait_recv()
 
+    early = len(started)
     column_a = r.reta.at[:, m, :, cols_a]
     row_b = r.reta.at[y, :, :, wide_b]
     tile_a, tile_b = r.reta.at[y, m, :, cols_a], r.reta.at[y, m, :, cols_b]
     ax, by = [], []
-    for j, (pa, pb) in enumerate(zip_longest(pairs(y, ys // 2), pairs(x, ms))):
+    count_y, wide_y, order_y = parts_of(y, ys)
+    count_x, wide_x, order_x = parts_of(x, xs)
+    for j, (pa, pb) in enumerate(zip_longest(order_y, order_x)):
         if pa is not None:
-            for source in [2 * pa, 2 * pa + 1] if j else [2 * pa + 1 - y % 2]:
+            for i in range(1 if j == 0 else 0, wide_y):
+                place = lax.rem(y + i, wide_y) if j == 0 else i
+                source = wide_y * pa + place
                 arrived("ay", tile_a, y, source, ys, at(yy=source))
-            region = r.reta.at[pl.ds(2 * pa, 2), m, :, cols_a]
+            region = r.reta.at[pl.ds(wide_y * pa, wide_y), m, :, cols_a]
             for k in kx:
                 ax.append((k, send(region, region, "ax", j * xs + k, at(xx=xp(k)))))
         if pb is not None:
-            for source in [2 * pb, 2 * pb + 1] if j else [2 * pb + 1 - x % 2]:
+            for i in range(1 if j == 0 else 0, wide_x):
+                place = lax.rem(x + i, wide_x) if j == 0 else i
+                source = wide_x * pb + place
                 arrived("bx_", tile_b, x, source, xs, at(xx=source))
-            region = r.reta.at[y, pb, :, wide_b]
+            region = r.reta.at[y, pl.ds(wide_x // 2 * pb, wide_x // 2), :, wide_b]
             for k in ky:
                 by.append((k, send(region, region, "by", j * ys + k, at(yy=yp(k)))))
     fa = [send(column_a, column_a, "fa", 0, sibling)]
     fb = [send(row_b, row_b, "fb", 0, sibling)]
-    for _, copy in bbx:
-        copy.wait_recv()
-    for s in range(nb):
-        total = r.bg[4 * s].astype(F32)
-        for i in range(1, 4):
-            total = total + r.bg[4 * s + i].astype(F32)
-        r.bt[y, s] = total.astype(BF16)
-    bby = [(k, send(r.bt.at[y], r.bt.at[y], "bby", k, at(yy=yp(k)))) for k in ky]
-
     r.g4r[q] = r.g4[q]
     for copy in ret:
         copy.wait_recv()
@@ -546,6 +572,9 @@
     turned = jnp.transpose(total)
     r.mixed[:, : T // 2] = (turned[:Q] + 0.25 * term[:, : T // 2]).astype(BF16)
     r.mixed[:, T // 2 :] = (turned[Q:] + 0.25 * term[:, T // 2 :]).astype(BF16)
+
+    for copy in started[:early]:
+        copy.wait_send()
 
     for k in kx:
         for other, copy in ax:
@@ -567,18 +596,16 @@
         fb.append(send(region, region, "fb", k, sibling))
     for _, copy in bby:
         copy.wait_recv()
-    bbs = send(r.bt, r.bs, "bbs", 0, sibling)
-    for copy in fa + fb:
-        copy.wait_recv()
-    bbs.wait_recv()
     for yy in range(ys):
         for s in range(nb):
-            both = r.bt[yy, s].astype(F32) + r.bs[yy, s].astype(F32)
+            both = r.bt[yy, s].astype(F32)
             row = (yy * ms + 2 * s) * RANK
             r.ball[row : row + RANK, :] = both
             r.ball[row + RANK : row + 2 * RANK, :] = pltpu.roll(both, Q, 1)
     r.retb[...] = jnp.transpose(r.ball[...])[:Q].astype(BF16)
-    for copy in started:
+    for copy in fa + fb:
+        copy.wait_recv()
+    for copy in started[early:]:
         copy.wait_send()
 
 

time: 69.9 us -> 69.2 us (0.990)
  Pallas kernels: 69.1 us -> 68.4 us
where the time goes in v3:
time: 69.2 us; the launch traced here: 69 us
  Pallas kernels  68.4 us (99%)
    pallas_call x1, Pallas kernels, shards(): pl.pallas_call(functools.partial(kernel, ys, xs, zs, order), out_shape=tu...  67.2 us

profile of v3, /device:TPU:1, one launch (start us, length us, event | category | flops | bytes accessed | tf_op | source)
XLA Modules:
  0.0 69.0 jit_solution(7081705401163846913)
XLA Ops:
  0.6 67.2 %shard_map.187 = (bf16[64,512]{1,0:T(8,128)(2,1)S(1)}, f32[4,1024]{1,0:T(4,128)S(1)}, f32[4,64]{1,0:T(4,128)S(1)}, f32[4,1024]{1,0:T(4,128)S(1)}, f32[4,1024]{1,...) custom-call(bf16[512,1024]{1,0:T(8,128)(2,1)} %refs_0_.1, ...), custom_call_target="tpu_custom_call" | custom-call | tf_op jit(solution)/shard_map/pallas_call | solution.py:632
  67.9 1.1 %shard_map.188 = (bf16[64,512]{1,0:T(8,128)(2,1)}, f32[4,1024]{1,0:T(4,128)}, f32[4,64]{1,0:T(4,128)}, f32[4,1024]{1,0:T(4,128)}, f32[4,1024]{1,0:T(4,128)}, /*i...) custom-call(bf16[64,512]{1,0:T(8,128)(2,1)S(1)} %get-tuple-element.27.refs_0_, ...), custom_call_target="tpu_custom_call" | custom-call | tf_op jit(solution)/shard_map/pallas_call | solution.py:642

commit v4 on v3

--- a/solution.py
+++ b/solution.py
@@ -306,6 +306,10 @@
             )
         )
 
+    cc.wait_recv()
+    r.c1[...] = r.c0[...] + r.c0r[...]
+    cx = [(k, send(r.c1, r.c1r.at[k], "cx", k, at(xx=xp(k)))) for k in kx]
+
     for _, copy in gz2:
         copy.wait_recv()
     spread_into(from_blocks(r.gg), r.spread_g)
@@ -317,6 +321,13 @@
     for part in range(2):
         columns = pl.ds(pl.multiple_of(half + part * 256, 256), 256)
         r.own[part] = jnp.dot(r.spread_g[...], r.tok[:, columns], preferred_element_type=F32)
+
+    total = r.c1[...]
+    for k, copy in cx:
+        copy.wait_recv()
+        total = total + r.c1r[k]
+    r.c2[...] = total
+    cy = [(k, send(r.c2, r.c2r.at[k], "cy", k, at(yy=yp(k)))) for k in ky]
 
     def chip_sum(part, yy, xx):
         rows = pl.ds(pl.multiple_of((yy * ms + xx // 2) * RANK, RANK), RANK)
@@ -363,9 +374,6 @@
             )
     sib.append(send(r.sbx, r.sbr, "sib", 2, sibling))
 
-    cc.wait_recv()
-    r.c1[...] = r.c0[...] + r.c0r[...]
-    cx = [(k, send(r.c1, r.c1r.at[k], "cx", k, at(xx=xp(k)))) for k in kx]
     sib[2].wait_recv()
     for yy in range(ys):
         for s in range(nb):
@@ -377,13 +385,6 @@
     pms = send(r.pm.at[core], r.pm.at[core], "pms", 0, sibling)
 
     base = [(k, send(r.bx.at[zp(k)], r.br.at[k], "bz", k, at(zz=zp(k)))) for k in kz]
-
-    total = r.c1[...]
-    for k, copy in cx:
-        copy.wait_recv()
-        total = total + r.c1r[k]
-    r.c2[...] = total
-    cy = [(k, send(r.c2, r.c2r.at[k], "cy", k, at(yy=yp(k)))) for k in ky]
 
     a2, b2 = [], []
     for g in range(SUM_PARTS):

time: 69.2 us -> 67.7 us (0.978)
  Pallas kernels: 68.4 us -> 66.9 us
    pallas_call x1, Pallas kernels: 67.2 us -> 65.8 us  [shards(): pl.pallas_call(functools.partial(kernel, ys, xs, zs, order), out_shape=tu...]
where the time goes in v4:
time: 67.7 us; the launch traced here: 67.6 us
  Pallas kernels  66.9 us (99%)
    pallas_call x1, Pallas kernels, shards(): pl.pallas_call(functools.partial(kernel, ys, xs, zs, order), out_shape=tu...  65.8 us

profile of v4, /device:TPU:1, one launch (start us, length us, event | category | flops | bytes accessed | tf_op | source)
XLA Modules:
  0.0 67.6 jit_solution(8555038840720875393)
XLA Ops:
  0.6 65.8 %shard_map.187 = (bf16[64,512]{1,0:T(8,128)(2,1)S(1)}, f32[4,1024]{1,0:T(4,128)S(1)}, f32[4,64]{1,0:T(4,128)S(1)}, f32[4,1024]{1,0:T(4,128)S(1)}, f32[4,1024]{1,...) custom-call(bf16[512,1024]{1,0:T(8,128)(2,1)} %refs_0_.1, ...), custom_call_target="tpu_custom_call" | custom-call | tf_op jit(solution)/shard_map/pallas_call | solution.py:633
  66.5 1.1 %shard_map.188 = (bf16[64,512]{1,0:T(8,128)(2,1)}, f32[4,1024]{1,0:T(4,128)}, f32[4,64]{1,0:T(4,128)}, f32[4,1024]{1,0:T(4,128)}, f32[4,1024]{1,0:T(4,128)}, /*i...) custom-call(bf16[64,512]{1,0:T(8,128)(2,1)S(1)} %get-tuple-element.27.refs_0_, ...), custom_call_target="tpu_custom_call" | custom-call | tf_op jit(solution)/shard_map/pallas_call | solution.py:643
